TPU v7x, 256 devices: a whole 4x4x8 slice. The times are simulated.
256 devices in a mesh: grp: 8 (over y, core), fsdp: 32 (over x, z).
Axes of the slice: x: 4, y: 4, z: 8, core: 2. Of those that a mesh axis runs over, the one named last changes fastest.
Arguments:
- grad_part: bfloat16 [8, 8, 16, 512, 512], P('grp', None, None, 'fsdp'), may hold values from -4 to 4
- adam_v: float32 [8, 16, 512, 512], P('grp', None, 'fsdp'), may hold values from 5e-07 to 4
- owner_of: int32 [8, 16, 1], P('grp'), may hold values from 0 to 31; in each aligned block of 16 rows (0 to 15, 16 to 31, ..., all dimensions but the last counted through in order) at most 2 rows name the same one
- gram_left: float32 [8, 32, 2, 512, 512], P('grp', 'fsdp'), may hold values from -0.25 to 12
- gram_right: float32 [8, 32, 2, 512, 512], P('grp', 'fsdp'), may hold values from -0.25 to 12
- root_left: bfloat16 [8, 32, 2, 512, 512], P('grp', 'fsdp'), may hold values from -0.1 to 1.2
- root_right: bfloat16 [8, 32, 2, 512, 512], P('grp', 'fsdp'), may hold values from -0.1 to 1.2
Outputs:
- update: bfloat16 [8, 16, 512, 512], P('grp', None, 'fsdp')
- gram_left_new: float32 [8, 32, 2, 512, 512], P('grp', 'fsdp')
- gram_right_new: float32 [8, 32, 2, 512, 512], P('grp', 'fsdp')
Inputs may be any that keep to these rules, and one draw needn't show every extreme that they name: `owner_of`: in each group, no owner is named by more than 2 of the group's 16 blocks, a bound that some block reaches.
All inputs are finite; a program needn't handle non-finite values.
Results may differ from a plain program's by a relative error of at most 0.022.
Values may be sent and summed in bfloat16 or wider, within the bound.
A program may use at most 64 MiB of HBM per device.

v0:
```python
import jax
import jax.numpy as jnp
from jax import lax
from jax.sharding import PartitionSpec as P

BETA2 = 0.9
EPS_ADAM = 1e-08
EPS_NORM = 1e-06
HIGHEST = lax.Precision.HIGHEST


def slot_numbers(owner_ids):
    count = owner_ids.shape[0]
    same = owner_ids[:, None] == owner_ids[None, :]
    order = jnp.arange(count, dtype=jnp.int32)
    earlier = order[None, :] < order[:, None]
    return jnp.sum(jnp.where(same & earlier, 1, 0), axis=1).astype(jnp.int32)


def per_device(grad_part, adam_v, owner_of, gram_left, gram_right, root_left, root_right):
    owner_count = lax.axis_size("fsdp")
    slot_count = gram_left.shape[2]
    block_order = gram_left.shape[3]
    replica_terms = grad_part[0].astype(jnp.float32)
    grad_sum = lax.psum_scatter(
        replica_terms.astype(jnp.bfloat16), "grp", scatter_dimension=0, tiled=True
    ).astype(jnp.float32)[0]
    second = BETA2 * adam_v[0] + (1.0 - BETA2) * grad_sum * grad_sum
    graft_dir = grad_sum / (jnp.sqrt(second) + EPS_ADAM)
    graft_part = jnp.sum(graft_dir * graft_dir, axis=(1, 2))
    owner_ids = owner_of[0, :, 0]
    slot_ids = slot_numbers(owner_ids)
    owner_range = jnp.arange(owner_count, dtype=jnp.int32)
    slot_range = jnp.arange(slot_count, dtype=jnp.int32)
    select = (
        (owner_ids[:, None, None] == owner_range[None, :, None])
        & (slot_ids[:, None, None] == slot_range[None, None, :])
    ).astype(jnp.float32)
    outgoing = jnp.einsum("jos,jrb->osrb", select, grad_sum, precision=HIGHEST)
    arrived = lax.all_to_all(
        outgoing.astype(jnp.bfloat16), "fsdp", split_axis=0, concat_axis=2, tiled=True
    ).astype(outgoing.dtype)
    owned_blocks = arrived[0]
    owned_bf = owned_blocks.astype(jnp.bfloat16)
    left_applied = jnp.einsum(
        "sab,sbc->sac", root_left[0, 0], owned_bf, preferred_element_type=jnp.float32
    ).astype(jnp.bfloat16)
    direction = jnp.einsum(
        "sab,sbc->sac", left_applied, root_right[0, 0], preferred_element_type=jnp.float32
    )
    row_pieces = direction.reshape(slot_count, owner_count, block_order // owner_count, block_order)
    graft_sq = lax.psum(graft_part, "fsdp")
    owner_sq = jnp.sum(direction * direction, axis=(1, 2))
    sq_copies = jnp.broadcast_to(owner_sq[:, None], (slot_count, owner_count))
    returned, sq_back = (
        lax.all_to_all(
            row_pieces.astype(jnp.bfloat16), "fsdp", split_axis=1, concat_axis=1, tiled=True
        ).astype(row_pieces.dtype),
        lax.all_to_all(
            sq_copies.astype(jnp.bfloat16), "fsdp", split_axis=1, concat_axis=1, tiled=True
        ).astype(sq_copies.dtype),
    )
    my_pieces = jnp.einsum("jos,sorb->jrb", select, returned, precision=HIGHEST)
    dir_sq = jnp.einsum("jos,so->j", select, sq_back, precision=HIGHEST)
    left_new = gram_left[0, 0] + jnp.einsum(
        "sab,scb->sac", owned_blocks, owned_blocks, precision=HIGHEST
    )
    right_new = gram_right[0, 0] + jnp.einsum(
        "sba,sbc->sac", owned_blocks, owned_blocks, precision=HIGHEST
    )
    scale = jnp.sqrt(graft_sq) / (jnp.sqrt(dir_sq) + EPS_NORM)
    update = (-scale[:, None, None] * my_pieces).astype(jnp.bfloat16)
    return (update[None], left_new[None, None], right_new[None, None])


def solution(mesh):
    placed = (
        P("grp", None, None, "fsdp", None),
        P("grp", None, "fsdp", None),
        P("grp", None, None),
        P("grp", "fsdp", None, None, None),
        P("grp", "fsdp", None, None, None),
        P("grp", "fsdp", None, None, None),
        P("grp", "fsdp", None, None, None),
    )
    return jax.shard_map(
        per_device,
        mesh=mesh,
        in_specs=placed,
        out_specs=(
            P("grp", None, "fsdp", None),
            P("grp", "fsdp", None, None, None),
            P("grp", "fsdp", None, None, None),
        ),
        check_vma=False,
    )
```

profile of v0, /device:TPU:24, one launch (start us, length us, event | category | flops | bytes accessed | tf_op | source)
XLA Modules:
  0.0 213.9 jit_solution(16037054995011317624)
XLA Ops:
  7.2 0.0 copy-start
  7.2 0.0 copy-start.3
  7.2 0.0 reduce-scatter.2.cloned.1.call-start
  7.2 0.7 reduce-scatter.2.cloned.1.call-update
  7.9 0.0 copy-done.3
  7.9 0.2 select_reduce_fusion
  8.1 0.1 iota_compare_fusion.1
  8.2 38.0 %reduce-scatter.2.cloned.1.call-done = bf16[1,16,16,512]{3,2,1,0:T(8,128)(2,1)} async-done(((bf16[8,16,16,512]{3,2,1,0:T(8,128)(2,1)}), bf16[1,16,16,512]{3,2,1,0:T(8,128)(2,1)}) %reduce-scatter.2.cloned.1.call-update) | async-done | bytes 262160 | tf_op jit(solution)/shard_map/reduce_scatter | solution.py:25
  46.2 1.5 convolution_convert_fusion.1
  47.7 0.6 copy.30
  48.3 38.3 %all_to_all.32 = bf16[32,2,16,512]{3,2,1,0:T(8,128)(2,1)S(1)} all-to-all(bf16[32,2,16,512]{3,2,1,0:T(8,128)(2,1)S(1)} %copy.30), channel_id=1, replica_groups=mesh['grp'=8,'fsdp'=32] {'fsdp'}, dimensions={0} | all-to-all | bytes 2097152 | tf_op jit(solution)/shard_map/all_to_all | solution.py:40
  86.5 0.1 copy.31
  86.6 0.0 copy-done
  86.6 2.8 %multiply_reduce_fusion = (bf16[2]{0:T(256)(128)(2,1)S(1)}, bf16[2,512,512]{2,1,0:T(8,128)(2,1)S(1)}) fusion(bf16[1,1,2,512,512]{4,3,2,1,0:T(8,128)(2,1)S(1)} %copy-done, bf16[2,512,512]{2,1,0:T(8,128)(2,1)S(1)} %bitcast.75, bf16[1,1,2,512,512]{4,3,2,1,0:T(8,128)(2,1)} %param.12), kind=kOutput, calls=%fused_computation.4 | convolution fusion | flops 1075838976 | bytes 4194308 | tf_op jit(solution)/shard_map/sab,sbc->sac/dot_general | solution.py:48
  89.4 0.6 broadcast_in_dim.31
  90.0 6.5 %all-to-all-start.1 = ((bf16[2,32,1]{0,2,1:T(2,128)(2,1)}), bf16[2,32,1]{0,2,1:T(2,128)(2,1)S(1)}, u32[]{:S(2)}, u32[]{:S(2)}) async-start(bf16[2,32,1]{0,2,1:T(2,128)(2,1)} %broadcast_in_dim.31), calls=%async_computation.2 | async-start | bytes 32768 | tf_op jit(solution)/shard_map/all_to_all | solution.py:59
  96.6 0.0 copy-start.2
  96.6 2.1 copy.35
  98.6 7.6 %all-to-all-done.1 = bf16[2,32,1]{0,2,1:T(2,128)(2,1)S(1)} async-done(((bf16[2,32,1]{0,2,1:T(2,128)(2,1)}), bf16[2,32,1]{0,2,1:T(2,128)(2,1)S(1)}, u32[]{:S(2)}, u32[]{:S(2)}) %all-to-all-start.1) | async-done | bytes 160 | tf_op jit(solution)/shard_map/all_to_all | solution.py:59
  106.3 3.9 %all-to-all-start.2 = ((bf16[2,32,16,512]{3,0,2,1:T(2,128)(2,1)}), bf16[2,32,16,512]{3,0,2,1:T(2,128)(2,1)S(1)}, u32[]{:S(2)}, u32[]{:S(2)}) async-start(bf16[2,32,16,512]{3,0,2,1:T(2,128)(2,1)} %copy.35), calls=%async_computation.3 | async-start | bytes 2097152 | tf_op jit(solution)/shard_map/all_to_all | solution.py:56
  110.2 0.0 copy-done.2
  110.2 1.5 fusion.18
  111.7 87.6 %psum.7 = f32[16]{0:T(128)S(1)} all-reduce(f32[16]{0:T(128)S(1)} %fusion.18), channel_id=1, replica_groups=mesh['grp'=8,'fsdp'=32] {'fsdp'}, use_global_device_ids=true, to_apply=%region_2.3 | all-reduce | flops 16 | bytes 128 | tf_op jit(solution)/shard_map/psum | solution.py:52
  199.3 0.0 copy-start.1
  199.3 3.8 %fusion = f32[1,1,2,512,512]{4,3,2,1,0:T(8,128)} fusion(f32[1,1,2,512,512]{4,3,2,1,0:T(8,128)} %param.11, bf16[2,512,512]{2,1,0:T(8,128)(2,1)S(1)} %bitcast.76), kind=kOutput, calls=%fused_computation.1 | convolution fusion | flops 537395200 | bytes 5242880 | tf_op jit(solution)/shard_map/sba,sbc->sac/dot_general | solution.py:68
  203.1 0.0 copy-done.1
  203.1 2.1 fusion.1
  205.2 0.1 copy.42
  205.3 0.2 fusion.9
  205.5 0.0 all-to-all-done.2
  205.5 0.7 fusion.5
  206.2 0.9 copy.38
  (1 shorter events, 0.0 us)
Async XLA Ops:
  7.2 79.5 %copy-start = (bf16[1,1,2,512,512]{4,3,2,1,0:T(8,128)(2,1)S(1)}, bf16[1,1,2,512,512]{4,3,2,1,0:T(8,128)(2,1)}, u32[]{:S(2)}) copy-start(bf16[1,1,2,512,512]{4,3,2,1,0:T(8,128)(2,1)} %param.13) | copy-start | bytes 3145732
  7.2 0.7 copy-start.3
  7.2 39.0 %reduce-scatter.2.cloned.1.call-start = ((), (), s32[]{:S(2)}) async-start(), calls=%async_computation.4 | async-start | bytes 2359296 | tf_op jit(solution)/shard_map/reduce_scatter | solution.py:25
  90.0 16.2 %all-to-all-start.1 = ((bf16[2,32,1]{0,2,1:T(2,128)(2,1)}), bf16[2,32,1]{0,2,1:T(2,128)(2,1)S(1)}, u32[]{:S(2)}, u32[]{:S(2)}) async-start(bf16[2,32,1]{0,2,1:T(2,128)(2,1)} %broadcast_in_dim.31), calls=%async_computation.2 | async-start | bytes 32768 | tf_op jit(solution)/shard_map/all_to_all | solution.py:59
  96.6 13.7 %copy-start.2 = (bf16[1,16,16,512]{3,2,1,0:T(8,128)(2,1)S(1)}, bf16[1,16,16,512]{3,2,1,0:T(8,128)(2,1)}, u32[]{:S(2)}) copy-start(bf16[1,16,16,512]{3,2,1,0:T(8,128)(2,1)} %reduce-scatter.2.cloned.1.call-done) | copy-start | bytes 786436
  106.3 99.2 %all-to-all-start.2 = ((bf16[2,32,16,512]{3,0,2,1:T(2,128)(2,1)}), bf16[2,32,16,512]{3,0,2,1:T(2,128)(2,1)S(1)}, u32[]{:S(2)}, u32[]{:S(2)}) async-start(bf16[2,32,16,512]{3,0,2,1:T(2,128)(2,1)} %copy.35), calls=%async_computation.3 | async-start | bytes 2097152 | tf_op jit(solution)/shard_map/all_to_all | solution.py:56
  199.3 3.8 %copy-start.1 = (f32[1,1,2,512,512]{4,3,2,1,0:T(8,128)S(1)}, f32[1,1,2,512,512]{4,3,2,1,0:T(8,128)}, u32[]{:S(2)}) copy-start(f32[1,1,2,512,512]{4,3,2,1,0:T(8,128)} %param.10) | copy-start | bytes 6291460
Sparse Core Ops, SparseCore 0:
  10.6 35.5 reduce-scatter.1
where the time goes:
time: 214 us
  blocking collectives  126 us (59%)
  waiting for transfers between devices  46.3 us (22%)
  between operations  14.1 us (7%)
  matrix products  11.1 us (5%)
  starting transfers between devices  10.5 us (5%)
  local copies, waits for them, and re-layouts  4.32 us (2%)
    psum x1, blocking collectives, per_device(): graft_sq = lax.psum(graft_part, 'fsdp')  87.6 us
    all_to_all x1, blocking collectives, per_device(): lax.all_to_all(outgoing.astype(jnp.bfloat16), 'fsdp', split_axis=0, conca...  38.3 us
    reduce_scatter x1, waiting for transfers between devices, per_device(): lax.psum_scatter(replica_terms.astype(jnp.bfloat16), 'grp', scatter_dimen...  38 us
    all_to_all x1, waiting for transfers between devices, per_device(): lax.all_to_all(sq_copies.astype(jnp.bfloat16), 'fsdp', split_axis=1, conc...  7.63 us
    all_to_all x1, starting transfers between devices, per_device(): lax.all_to_all(sq_copies.astype(jnp.bfloat16), 'fsdp', split_axis=1, conc...  6.52 us
  transfers between devices with their start and end apart: 3, of which 2 were waited for; matrix products, arithmetic and copies ran while one was open for 5% of the time, Pallas kernels for 0%

commit v1 on v0

v1 whole, which is shorter than its diff:
```python
import functools

import jax
import jax.numpy as jnp
from jax import lax
from jax.experimental import pallas as pl
from jax.experimental.pallas import tpu as pltpu
from jax.sharding import PartitionSpec as P

BETA2 = 0.9
EPS_ADAM = 1e-08
EPS_NORM = 1e-06
MESH = pl.DeviceIdType.MESH

NX, NY, NZ = 4, 4, 8
BLOCKS, ROWS, ORDER, SLOTS = 16, 16, 512, 2
PARTS = 4
COLS = ORDER // PARTS
CAPS = (8,)

T_LIST, T_PLACE, T_OWNED, T_PLANE, T_RANK, T_MINE, T_HELD = 0, 64, 72, 80, 96, 112, 114


def position():
    g = lax.axis_index("grp")
    f = lax.axis_index("fsdp")
    return g, f, g // 2, g % 2, f // NZ, f % NZ


def remote(src, dst, send, recv, device):
    return pltpu.make_async_remote_copy(
        src_ref=src, dst_ref=dst, send_sem=send, recv_sem=recv,
        device_id=device, device_id_type=MESH,
    )


def pair_kernel(parts_ref, load_ref, out_ref, most_ref, own, other, loads, own_sem, send, recv, lsend, lrecv):
    g, f, y, c, x, z = position()
    own_copies = []
    for i in range(NY):
        copy = pltpu.make_async_copy(parts_ref.at[0, i * 2 + c], own.at[i], own_sem.at[i])
        copy.start()
        own_copies.append(copy)
    barrier = pltpu.get_barrier_semaphore()
    for d in range(1, 8):
        pl.semaphore_signal(barrier, inc=1, device_id=((g + d) % 8, f), device_id_type=MESH)
    pl.semaphore_wait(barrier, 7)
    load_copies = []
    for d in range(1, 8):
        copy = remote(load_ref, loads.at[d], lsend.at[d], lrecv.at[d], ((g + d) % 8, f))
        copy.start()
        load_copies.append(copy)
    copies = []
    for i in range(NY):
        copy = remote(parts_ref.at[0, i * 2 + 1 - c], other.at[i], send.at[i], recv.at[i], (y * 2 + 1 - c, f))
        copy.start()
        copies.append(copy)
    for i in range(NY):
        own_copies[i].wait()
        copies[i].wait_recv()
        for p in range(PARTS):
            cols = pl.ds(p * COLS, COLS)
            total = own[i, :, :, cols].astype(jnp.float32) + other[i, :, :, cols].astype(jnp.float32)
            out_ref[p, i] = total.astype(jnp.bfloat16)
    most = load_ref[...]
    for d in range(1, 8):
        load_copies[d - 1].wait_recv()
        most = jnp.maximum(most, loads[d])
    most_ref[...] = most
    for copy in load_copies + copies:
        copy.wait_send()


def pair_sum(grad_part, load):
    return pl.pallas_call(
        pair_kernel,
        out_shape=(
            jax.ShapeDtypeStruct((PARTS, NY, BLOCKS, ROWS, COLS), jnp.bfloat16),
            jax.ShapeDtypeStruct((8, 128), jnp.float32),
        ),
        in_specs=[pl.BlockSpec(memory_space=pl.ANY), pl.BlockSpec(memory_space=pltpu.VMEM)],
        out_specs=(pl.BlockSpec(memory_space=pltpu.VMEM), pl.BlockSpec(memory_space=pltpu.VMEM)),
        scratch_shapes=[
            pltpu.VMEM((NY, BLOCKS, ROWS, ORDER), jnp.bfloat16),
            pltpu.VMEM((NY, BLOCKS, ROWS, ORDER), jnp.bfloat16),
            pltpu.VMEM((8, 8, 128), jnp.float32),
            pltpu.SemaphoreType.DMA((NY,)),
            pltpu.SemaphoreType.DMA((NY,)),
            pltpu.SemaphoreType.DMA((NY,)),
            pltpu.SemaphoreType.DMA((8,)),
            pltpu.SemaphoreType.DMA((8,)),
        ],
        compiler_params=pltpu.CompilerParams(
            collective_id=0, has_side_effects=True, vmem_limit_bytes=32 << 20
        ),
        name="pair_sum",
    )(grad_part, load)


def step_kernel(cap, tbl, pairs, adam_hbm, gl_hbm, gr_hbm, rl_hbm, rr_hbm,
                upd, gl_out, gr_out, *scratch):
    scratch = list(scratch)
    take = lambda n: [scratch.pop(0) for _ in range(n)]
    gbf, zsend, zrecv, xret, zback, zret = (take(PARTS) for _ in range(6))
    (yown, yrecv, gsum, xsend, xrecv, gmat, dirb, xback, adam, gl, gr, rl, rr,
     gpart, gzrecv, gzsum, gxrecv,
     lsem, ysem, ysend_sem, yrecv_sem, zsend_sem, zrecv_sem, xsend_sem, xrecv_sem,
     bxsend_sem, bxrecv_sem, bzsend_sem, bzrecv_sem, gsend_sem, grecv_sem, osem) = scratch
    g, f, y, c, x, z = position()
    at_y = lambda i: (i * 2 + c, f)
    at_z = lambda i: (g, x * NZ + i)
    at_x = lambda i: (g, i * NZ + z)
    plus = lambda a, d, n: (a + d) % n
    sends = []

    def start(copy):
        copy.start()
        sends.append(copy)
        return copy

    own_copies = []
    for p in range(PARTS):
        copy = pltpu.make_async_copy(pairs.at[p, y], yown.at[p], ysem.at[p])
        copy.start()
        own_copies.append(copy)
    big = []
    for i, (src, dst) in enumerate(((adam_hbm.at[0], adam), (rl_hbm.at[0, 0], rl), (rr_hbm.at[0, 0], rr),
                                    (gl_hbm.at[0, 0], gl), (gr_hbm.at[0, 0], gr))):
        copy = pltpu.make_async_copy(src, dst, lsem.at[i])
        copy.start()
        big.append(copy)

    barrier = pltpu.get_barrier_semaphore()
    partners = (
        [at_y(plus(y, d, NY)) for d in range(1, NY)]
        + [at_z(plus(z, d, NZ)) for d in range(1, NZ)]
        + [at_x(plus(x, d, NX)) for d in range(1, NX)]
    )
    for partner in partners:
        pl.semaphore_signal(barrier, inc=1, device_id=partner, device_id_type=MESH)
    pl.semaphore_wait(barrier, len(partners))

    y_copies = [[] for _ in range(PARTS)]
    for p in range(PARTS):
        for d in range(1, NY):
            to = plus(y, d, NY)
            y_copies[p].append(start(remote(
                pairs.at[p, to], yrecv.at[p, d - 1], ysend_sem.at[p * 3 + d - 1], yrecv_sem.at[p * 3 + d - 1], at_y(to))))

    z_copies = [[] for _ in range(PARTS)]
    x_copies = [[] for _ in range(PARTS)]
    bx_copies = [[] for _ in range(PARTS)]
    bz_copies = [[] for _ in range(PARTS)]

    def reduce_part(p):
        own_copies[p].wait()
        for copy in y_copies[p]:
            copy.wait_recv()
        total = yown[p].astype(jnp.float32)
        for d in range(NY - 1):
            total = total + yrecv[p, d].astype(jnp.float32)
        gsum[p] = total
        gbf[p][...] = total.astype(jnp.bfloat16)

        @pl.loop(0, NZ)
        def _(i):
            for k in range(cap):
                zsend[p][i, k] = gbf[p][tbl[T_LIST + i * 8 + k]]

        for d in range(1, NZ):
            to = plus(z, d, NZ)
            n = p * 7 + d - 1
            z_copies[p].append(start(remote(
                zsend[p].at[to], zrecv[p].at[z], zsend_sem.at[n], zrecv_sem.at[n], at_z(to))))
        zrecv[p][z] = zsend[p][z]

    def pass_on(p):
        for copy in z_copies[p]:
            copy.wait_recv()

        for i in range(NX * SLOTS):
            k = tbl[T_PLACE + i]
            for r in range(NZ):
                xsend[p, i // SLOTS, i % SLOTS, r] = zrecv[p][r, k]

        for d in range(1, NX):
            to = plus(x, d, NX)
            n = p * 3 + d - 1
            x_copies[p].append(start(remote(
                xsend.at[p, to], xrecv.at[p, x], xsend_sem.at[n], xrecv_sem.at[n], at_x(to))))
        xrecv[p, x] = xsend[p, x]

    def apply_roots(p):
        for copy in x_copies[p]:
            copy.wait_recv()

        @pl.loop(0, SLOTS)
        def _(s):
            block = xrecv[p, :, s].reshape(ORDER, COLS)
            gmat[s, :, p * COLS:(p + 1) * COLS] = block
            left = jnp.dot(rl[s], block, preferred_element_type=jnp.float32).astype(jnp.bfloat16)
            term = jnp.dot(left, rr[s, p * COLS:(p + 1) * COLS, :], preferred_element_type=jnp.float32)
            if p == 0:
                dirb[s] = term
            else:
                dirb[s] += term

    graft_z = []
    graft_x = []

    def graft_first():
        big[0].wait()
        part = jnp.zeros((BLOCKS, COLS), jnp.float32)
        for p in range(PARTS):
            total = gsum[p]
            second = BETA2 * adam[:, :, p * COLS:(p + 1) * COLS] + (1.0 - BETA2) * total * total
            ratio = total / (jnp.sqrt(second) + EPS_ADAM)
            part = part + jnp.sum(ratio * ratio, axis=1)
        gpart[...] = part
        for d in range(1, NZ):
            graft_z.append(start(remote(
                gpart, gzrecv.at[d - 1], gsend_sem.at[d - 1], grecv_sem.at[d - 1], at_z(plus(z, d, NZ)))))

    def graft_second():
        total = gpart[...]
        for d in range(NZ - 1):
            graft_z[d].wait_recv()
            total = total + gzrecv[d]
        gzsum[...] = total
        for d in range(1, NX):
            n = 6 + d
            graft_x.append(start(remote(
                gzsum, gxrecv.at[d - 1], gsend_sem.at[n], grecv_sem.at[n], at_x(plus(x, d, NX)))))

    reduce_part(0)
    reduce_part(1)
    pass_on(0)
    reduce_part(2)
    pass_on(1)
    reduce_part(3)
    graft_first()
    big[1].wait()
    big[2].wait()
    apply_roots(0)
    pass_on(2)
    graft_second()
    apply_roots(1)
    pass_on(3)
    apply_roots(2)
    graft = gzsum[...]
    for d in range(NX - 1):
        graft_x[d].wait_recv()
        graft = graft + gxrecv[d]
    block_ids = lax.broadcasted_iota(jnp.int32, (BLOCKS, COLS), 0)
    graft_norms = []
    for s in range(SLOTS):
        graft_norms.append(jnp.sqrt(jnp.sum(jnp.where(block_ids == tbl[T_MINE + s], graft, 0.0), keepdims=True)))
    apply_roots(3)

    for s in range(SLOTS):
        whole = dirb[s]
        norm = jnp.sqrt(jnp.sum(whole * whole, keepdims=True))
        scale = -(graft_norms[s] / (norm + EPS_NORM))
        for p in range(PARTS):
            piece = (whole[:, p * COLS:(p + 1) * COLS] * scale).astype(jnp.bfloat16)
            xback[p, :, s] = piece.reshape(NX, NZ, ROWS, COLS)
    for p in range(PARTS):
        for d in range(1, NX):
            to = plus(x, d, NX)
            n = p * 3 + d - 1
            bx_copies[p].append(start(remote(
                xback.at[p, to], xret[p].at[x], bxsend_sem.at[n], bxrecv_sem.at[n], at_x(to))))
        xret[p][x] = xback[p, x]

    big[3].wait()
    big[4].wait()

    @pl.loop(0, SLOTS)
    def _(s):
        held = tbl[T_HELD + s] > 0
        block = gmat[s]
        outer = lax.dot_general(block, block, (((1,), (1,)), ((), ())), preferred_element_type=jnp.float32)
        gl[s] = gl[s] + jnp.where(held, outer, 0.0)
        outer = lax.dot_general(block, block, (((0,), (0,)), ((), ())), preferred_element_type=jnp.float32)
        gr[s] = gr[s] + jnp.where(held, outer, 0.0)

    out_copies = [
        pltpu.make_async_copy(gl, gl_out.at[0, 0], osem.at[0]),
        pltpu.make_async_copy(gr, gr_out.at[0, 0], osem.at[1]),
    ]
    for copy in out_copies:
        copy.start()

    def pass_back(p):
        for copy in bx_copies[p]:
            copy.wait_recv()

        for k in range(cap):
            e = tbl[T_OWNED + k]
            for r in range(NZ):
                zback[p][r, k] = xret[p][e // SLOTS, e % SLOTS, r]

        for d in range(1, NZ):
            to = plus(z, d, NZ)
            n = p * 7 + d - 1
            bz_copies[p].append(start(remote(
                zback[p].at[to], zret[p].at[z], bzsend_sem.at[n], bzrecv_sem.at[n], at_z(to))))
        zret[p][z] = zback[p][z]

    def finish(p):
        for copy in bz_copies[p]:
            copy.wait_recv()
        for j in range(BLOCKS):
            upd[0, j, :, p * COLS:(p + 1) * COLS] = zret[p][tbl[T_PLANE + j], tbl[T_RANK + j]]

    for p in range(PARTS):
        pass_back(p)
    for p in range(PARTS):
        finish(p)
    for copy in out_copies:
        copy.wait()
    for copy in sends:
        copy.wait_send()


def step(cap, collective_id, tbl, pairs, adam_v, gram_left, gram_right, root_left, root_right):
    tile = (ROWS, COLS)
    bf, f32 = jnp.bfloat16, jnp.float32
    vm = pltpu.VMEM
    dma = pltpu.SemaphoreType.DMA
    scratch = (
        [vm((BLOCKS,) + tile, bf)] * PARTS
        + [vm((NZ, cap) + tile, bf)] * PARTS
        + [vm((NZ, cap) + tile, bf)] * PARTS
        + [vm((NX, SLOTS, NZ) + tile, bf)] * PARTS
        + [vm((NZ, cap) + tile, bf)] * PARTS
        + [vm((NZ, cap) + tile, bf)] * PARTS
        + [
            vm((PARTS, BLOCKS) + tile, bf),
            vm((PARTS, NY - 1, BLOCKS) + tile, bf),
            vm((PARTS, BLOCKS) + tile, f32),
            vm((PARTS, NX, SLOTS, NZ) + tile, bf),
            vm((PARTS, NX, SLOTS, NZ) + tile, bf),
            vm((SLOTS, ORDER, ORDER), bf),
            vm((SLOTS, ORDER, ORDER), f32),
            vm((PARTS, NX, SLOTS, NZ) + tile, bf),
            vm((BLOCKS, ROWS, ORDER), f32),
            vm((SLOTS, ORDER, ORDER), f32),
            vm((SLOTS, ORDER, ORDER), f32),
            vm((SLOTS, ORDER, ORDER), bf),
            vm((SLOTS, ORDER, ORDER), bf),
            vm((BLOCKS, COLS), f32),
            vm((NZ - 1, BLOCKS, COLS), f32),
            vm((BLOCKS, COLS), f32),
            vm((NX - 1, BLOCKS, COLS), f32),
            dma((5,)), dma((PARTS,)),
            dma((PARTS * 3,)), dma((PARTS * 3,)),
            dma((PARTS * 7,)), dma((PARTS * 7,)),
            dma((PARTS * 3,)), dma((PARTS * 3,)),
            dma((PARTS * 3,)), dma((PARTS * 3,)),
            dma((PARTS * 7,)), dma((PARTS * 7,)),
            dma((10,)), dma((10,)), dma((2,)),
        ]
    )
    hbm = pl.BlockSpec(memory_space=pl.ANY)
    return pl.pallas_call(
        functools.partial(step_kernel, cap),
        out_shape=(
            jax.ShapeDtypeStruct((1, BLOCKS, ROWS, ORDER), bf),
            jax.ShapeDtypeStruct(gram_left.shape, f32),
            jax.ShapeDtypeStruct(gram_right.shape, f32),
        ),
        in_specs=[pl.BlockSpec(memory_space=pltpu.SMEM)] + [hbm] * 6,
        out_specs=(pl.BlockSpec(memory_space=pltpu.VMEM), hbm, hbm),
        scratch_shapes=scratch,
        compiler_params=pltpu.CompilerParams(
            collective_id=collective_id, has_side_effects=True, vmem_limit_bytes=48 << 20
        ),
        name=f"step_{cap}",
    )(tbl, pairs, adam_v, gram_left, gram_right, root_left, root_right)


def index_table(owner_ids):
    me = lax.axis_index("fsdp")
    iota = lambda n: jnp.arange(n, dtype=jnp.int32)
    order = iota(BLOCKS)
    earlier = order[None, :] < order[:, None]
    plane, line = owner_ids % NZ, owner_ids // NZ
    count = lambda same: jnp.sum(jnp.where(same & earlier, 1, 0), axis=1).astype(jnp.int32)
    slot = count(owner_ids[:, None] == owner_ids[None, :])
    rank = count(plane[:, None] == plane[None, :])
    pick = lambda where, value: jnp.sum(jnp.where(where, value, 0), axis=-1).astype(jnp.int32).reshape(-1)
    listed = pick((plane == iota(NZ)[:, None, None]) & (rank == iota(8)[None, :, None]), order)
    owners = iota(NX)[:, None, None] * NZ + me % NZ
    place = pick((owner_ids == owners) & (slot == iota(SLOTS)[None, :, None]), rank)
    owned = pick((plane == me % NZ) & (rank == iota(8)[:, None]), line * SLOTS + slot)
    is_mine = (owner_ids == me) & (slot == iota(SLOTS)[:, None])
    mine = pick(is_mine, order)
    held = pick(is_mine, 1)
    table = jnp.concatenate([listed, place, owned, plane, rank, mine, held, jnp.zeros((12,), jnp.int32)])
    return table, jnp.max(rank) + 1


def per_device(grad_part, adam_v, owner_of, gram_left, gram_right, root_left, root_right):
    table, load = index_table(owner_of[0, :, 0])
    load = jnp.broadcast_to(load.astype(jnp.float32), (8, 128))
    pairs, most = pair_sum(grad_part, load)
    operands = (table, pairs, adam_v, gram_left, gram_right, root_left, root_right)
    if len(CAPS) == 1:
        return step(CAPS[0], 1, *operands)
    most = most[0, 0]
    which = sum((most > cap).astype(jnp.int32) for cap in CAPS[:-1])
    branches = [functools.partial(step, cap, i + 1) for i, cap in enumerate(CAPS)]
    return lax.switch(which, branches, *operands)


def solution(mesh):
    placed = (
        P("grp", None, None, "fsdp", None),
        P("grp", None, "fsdp", None),
        P("grp", None, None),
        P("grp", "fsdp", None, None, None),
        P("grp", "fsdp", None, None, None),
        P("grp", "fsdp", None, None, None),
        P("grp", "fsdp", None, None, None),
    )
    return jax.shard_map(
        per_device,
        mesh=mesh,
        in_specs=placed,
        out_specs=(
            P("grp", None, "fsdp", None),
            P("grp", "fsdp", None, None, None),
            P("grp", "fsdp", None, None, None),
        ),
        check_vma=False,
    )
```

time: 214 us -> 99 us (0.46)
  the two profiles are of different devices: /device:TPU:24 before, /device:TPU:4 now
where the time goes in v1:
time: 99 us; the launch traced here: 97.6 us
  Pallas kernels  84.4 us (85%)
  local copies, waits for them, and re-layouts  7.35 us (7%)
  other arithmetic  4.46 us (5%)
  between operations  1.37 us (1%)
    pallas_call x1, Pallas kernels, step(): pl.pallas_call(functools.partial(step_kernel, cap), out_shape=(jax.ShapeD...  77.3 us
    pallas_call x1, Pallas kernels, pair_sum(): pl.pallas_call(pair_kernel, out_shape=(jax.ShapeDtypeStruct((PARTS, NY, B...  7.15 us
    unnamed x13, local copies, waits for them, and re-layouts  7.01 us

profile of v1, /device:TPU:4, one launch (start us, length us, event | category | flops | bytes accessed | tf_op | source)
XLA Modules:
  0.0 97.6 jit_solution(4890700608707746036)
XLA Ops:
  0.6 0.9 select_reduce_fusion.1
  1.6 0.7 multiply_add_fusion
  2.2 0.7 broadcast_compare_fusion
  3.0 0.7 broadcast_compare_fusion.2
  3.6 0.2 select_reduce_fusion.2
  3.8 0.6 reduce_max.9
  5.1 0.1 select_reduce_fusion.3
  5.2 0.1 select_reduce_fusion.4
  5.4 0.2 fusion.3
  5.5 0.1 copy.10
  5.6 0.1 reshape.204
  5.7 0.2 select_reduce_fusion
  6.0 0.1 reshape.203
  6.0 0.1 concatenate.3.tbl
  6.1 0.0 copy-start
  6.1 1.6 %copy-done = bf16[1,8,16,16,512]{4,3,2,1,0:T(8,128)(2,1)S(1)} copy-done((bf16[1,8,16,16,512]{4,3,2,1,0:T(8,128)(2,1)S(1)}, bf16[1,8,16,16,512]{4,3,2,1,0:T(8,128)(2,1)}, u32[]{:S(2)}) %copy-start) | copy-done | bytes 2097176
  7.7 0.0 copy-start.1
  7.7 0.0 copy-start.2
  7.7 7.2 %pair_sum.1 = (bf16[4,4,16,16,128]{4,3,2,1,0:T(8,128)(2,1)S(1)}, f32[8,128]{1,0:T(8,128)}) custom-call(bf16[1,8,16,16,512]{4,3,2,1,0:T(8,128)(2,1)S(1)} %copy-done, f32[8,128]{1,0:T(8,128)S(1)} %broadcast_in_dim.79.load_ref), custom_call_target="tpu_custom_call" | custom-call | tf_op jit(solution)/shard_map/pair_sum/pallas_call | solution.py:75
  14.9 0.0 copy-done.1
  14.9 0.0 copy-done.2
  14.9 0.0 copy-start.3
  14.9 1.0 %copy-done.3 = f32[1,16,16,512]{3,2,1,0:T(8,128)S(1)} copy-done((f32[1,16,16,512]{3,2,1,0:T(8,128)S(1)}, f32[1,16,16,512]{3,2,1,0:T(8,128)}, u32[]{:S(2)}) %copy-start.3) | copy-done | bytes 524312
  15.9 77.3 %step_8.1 = (bf16[1,16,16,512]{3,2,1,0:T(8,128)(2,1)S(1)}, f32[1,1,2,512,512]{4,3,2,1,0:T(8,128)S(1)}, f32[1,1,2,512,512]{4,3,2,1,0:T(8,128)}) custom-call(s32[128]{0:T(128)S(1)} %concatenate.3.tbl, bf16[4,4,16,16,128]{4,3,2,1,0:T(8,128)(2,1)S(1)} %get-tuple-element.4.pairs, f32[1,16,16,512]{3,2,1,0:T(8,128)S(1)} %copy-done.3, ...), custom_call_target="tpu_custom_call" | custom-call | tf_op jit(solution)/shard_map/step_8/pallas_call | solution.py:366
  93.2 0.7 copy.14
  93.9 0.0 copy-start.4
  93.9 1.3 %copy.15 = f32[1,1,2,512,512]{4,3,2,1,0:T(8,128)} copy(f32[1,1,2,512,512]{4,3,2,1,0:T(8,128)S(1)} %get-tuple-element.16) | data formatting | bytes 4194304
  95.2 1.0 %copy-done.4 = f32[1,1,2,512,512]{4,3,2,1,0:T(8,128)S(1)} copy-done((f32[1,1,2,512,512]{4,3,2,1,0:T(8,128)S(1)}, f32[1,1,2,512,512]{4,3,2,1,0:T(8,128)}, u32[]{:S(2)}) %copy-start.4) | copy-done | bytes 2097176
  96.3 1.3 %copy.16 = f32[1,1,2,512,512]{4,3,2,1,0:T(8,128)} copy(f32[1,1,2,512,512]{4,3,2,1,0:T(8,128)S(1)} %copy-done.4) | data formatting | bytes 4194304
  (5 shorter events, 0.0 us)
Async XLA Ops:
  6.1 1.6 %copy-start = (bf16[1,8,16,16,512]{4,3,2,1,0:T(8,128)(2,1)S(1)}, bf16[1,8,16,16,512]{4,3,2,1,0:T(8,128)(2,1)}, u32[]{:S(2)}) copy-start(bf16[1,8,16,16,512]{4,3,2,1,0:T(8,128)(2,1)} %parts_ref.1) | copy-start | bytes 6291460
  7.7 7.2 %copy-start.1 = (bf16[1,1,2,512,512]{4,3,2,1,0:T(8,128)(2,1)S(1)}, bf16[1,1,2,512,512]{4,3,2,1,0:T(8,128)(2,1)}, u32[]{:S(2)}) copy-start(bf16[1,1,2,512,512]{4,3,2,1,0:T(8,128)(2,1)} %rl_hbm.1) | copy-start | bytes 3145732
  7.7 7.2 %copy-start.2 = (bf16[1,1,2,512,512]{4,3,2,1,0:T(8,128)(2,1)S(1)}, bf16[1,1,2,512,512]{4,3,2,1,0:T(8,128)(2,1)}, u32[]{:S(2)}) copy-start(bf16[1,1,2,512,512]{4,3,2,1,0:T(8,128)(2,1)} %rr_hbm.1) | copy-start | bytes 3145732
  14.9 1.0 %copy-start.3 = (f32[1,16,16,512]{3,2,1,0:T(8,128)S(1)}, f32[1,16,16,512]{3,2,1,0:T(8,128)}, u32[]{:S(2)}) copy-start(f32[1,16,16,512]{3,2,1,0:T(8,128)} %adam_hbm.1) | copy-start | bytes 1572868
  93.9 2.3 %copy-start.4 = (f32[1,1,2,512,512]{4,3,2,1,0:T(8,128)S(1)}, f32[1,1,2,512,512]{4,3,2,1,0:T(8,128)}, u32[]{:S(2)}) copy-start(f32[1,1,2,512,512]{4,3,2,1,0:T(8,128)} %get-tuple-element.17) | copy-start | bytes 6291460

commit v2 on v1

v2 whole, which is shorter than its diff:
```python
import functools

import jax
import jax.numpy as jnp
from jax import lax
from jax.experimental import pallas as pl
from jax.experimental.pallas import tpu as pltpu
from jax.sharding import PartitionSpec as P

BETA2 = 0.9
EPS_ADAM = 1e-08
EPS_NORM = 1e-06
MESH = pl.DeviceIdType.MESH

NX, NY, NZ = 4, 4, 8
BLOCKS, ROWS, ORDER, SLOTS = 16, 16, 512, 2
PARTS = 4
COLS = ORDER // PARTS
CAPS = (4, 5, 8)
CHUNKS = 4
BACK_ORDER = (4, 3, 5, 2, 6, 1, 7, 0)

T_LIST, T_PLACE, T_OWNED, T_PLANE, T_RANK, T_MINE, T_HELD = 0, 64, 72, 80, 96, 112, 114


def position():
    g = lax.axis_index("grp")
    f = lax.axis_index("fsdp")
    return g, f, g // 2, g % 2, f // NZ, f % NZ


def remote(src, dst, send, recv, device):
    return pltpu.make_async_remote_copy(
        src_ref=src, dst_ref=dst, send_sem=send, recv_sem=recv,
        device_id=device, device_id_type=MESH,
    )


def index_table(owner_ref, me, z):
    shape = (BLOCKS, 128)
    row = lax.broadcasted_iota(jnp.int32, shape, 0)
    lane = lax.broadcasted_iota(jnp.int32, shape, 1)
    down = jnp.zeros(shape, jnp.int32)
    across = jnp.zeros(shape, jnp.int32)
    for j in range(BLOCKS):
        down = jnp.where(row == j, owner_ref[j], down)
        across = jnp.where(lane == j, owner_ref[j], across)
    count = lambda same: jnp.sum(jnp.where(same & (lane < row), 1.0, 0.0), axis=1, keepdims=True)
    slot = count(down == across).astype(jnp.int32)
    ranks = count(down % NZ == across % NZ)
    rank = ranks.astype(jnp.int32)
    plane, line = down % NZ, down // NZ
    here = plane == z
    mine = down == me
    whole = jnp.zeros(shape, jnp.int32)
    for first, size, cond, value in (
        (T_LIST, 64, lambda e: (plane == e // 8) & (rank == e % 8), row),
        (T_PLACE, 8, lambda e: here & (line == e // SLOTS) & (slot == e % SLOTS), rank),
        (T_OWNED, 8, lambda e: here & (rank == e), line * SLOTS + slot),
        (T_PLANE, 16, lambda e: row == e, plane),
        (T_RANK, 16, lambda e: row == e, rank),
        (T_MINE, 2, lambda e: mine & (slot == e), row),
        (T_HELD, 2, lambda e: mine & (slot == e), 1),
    ):
        entry = lane - first
        whole += jnp.where((entry >= 0) & (entry < size) & cond(entry), value, 0)
    table = jnp.sum(whole.astype(jnp.float32), axis=0, keepdims=True).astype(jnp.int32)
    return table, jnp.max(ranks, keepdims=True) + 1.0


def pair_kernel(parts_ref, owner_ref, out_ref, tbl_ref, which_ref,
                own, other, load, loads, own_sem, send, recv, lsend, lrecv):
    g, f, y, c, x, z = position()
    own_copies = []
    for i in range(NY):
        copy = pltpu.make_async_copy(parts_ref.at[0, i * 2 + c], own.at[i], own_sem.at[i])
        copy.start()
        own_copies.append(copy)
    barrier = pltpu.get_barrier_semaphore()
    for d in range(1, 8):
        pl.semaphore_signal(barrier, inc=1, device_id=((g + d) % 8, f), device_id_type=MESH)
    table, most = index_table(owner_ref, f, z)
    tbl_ref[...] = jnp.broadcast_to(table, (8, 128))
    load[...] = jnp.broadcast_to(most, (8, 128))
    pl.semaphore_wait(barrier, 7)
    copies = []
    for i in range(NY):
        copy = remote(parts_ref.at[0, i * 2 + 1 - c], other.at[i], send.at[i], recv.at[i], (y * 2 + 1 - c, f))
        copy.start()
        copies.append(copy)
    load_copies = []
    for d in range(1, 8):
        copy = remote(load, loads.at[d], lsend.at[d], lrecv.at[d], ((g + d) % 8, f))
        copy.start()
        load_copies.append(copy)
    for i in range(NY):
        own_copies[i].wait()
        copies[i].wait_recv()
        for p in range(PARTS):
            cols = pl.ds(p * COLS, COLS)
            total = own[i, :, :, cols].astype(jnp.float32) + other[i, :, :, cols].astype(jnp.float32)
            out_ref[p, i] = total.astype(jnp.bfloat16)
    most = load[...]
    for d in range(1, 8):
        load_copies[d - 1].wait_recv()
        most = jnp.maximum(most, loads[d])
    most = jnp.max(most)
    which_ref[0] = sum((most > cap).astype(jnp.int32) for cap in CAPS[:-1])
    for copy in load_copies + copies:
        copy.wait_send()


def pair_sum(grad_part, owner_ids):
    return pl.pallas_call(
        pair_kernel,
        out_shape=(
            jax.ShapeDtypeStruct((PARTS, NY, BLOCKS, ROWS, COLS), jnp.bfloat16),
            jax.ShapeDtypeStruct((8, 128), jnp.int32),
            jax.ShapeDtypeStruct((1,), jnp.int32),
        ),
        in_specs=[pl.BlockSpec(memory_space=pl.ANY), pl.BlockSpec(memory_space=pltpu.SMEM)],
        out_specs=(
            pl.BlockSpec(memory_space=pltpu.VMEM),
            pl.BlockSpec(memory_space=pltpu.VMEM),
            pl.BlockSpec(memory_space=pltpu.SMEM),
        ),
        scratch_shapes=[
            pltpu.VMEM((NY, BLOCKS, ROWS, ORDER), jnp.bfloat16),
            pltpu.VMEM((NY, BLOCKS, ROWS, ORDER), jnp.bfloat16),
            pltpu.VMEM((8, 128), jnp.float32),
            pltpu.VMEM((8, 8, 128), jnp.float32),
            pltpu.SemaphoreType.DMA((NY,)),
            pltpu.SemaphoreType.DMA((NY,)),
            pltpu.SemaphoreType.DMA((NY,)),
            pltpu.SemaphoreType.DMA((8,)),
            pltpu.SemaphoreType.DMA((8,)),
        ],
        compiler_params=pltpu.CompilerParams(
            collective_id=0, has_side_effects=True, vmem_limit_bytes=60 << 20
        ),
        name="pair_sum",
    )(grad_part, owner_ids)


def step_kernel(cap, tbl_hbm, pairs, adam_hbm, gl_hbm, gr_hbm, rl_hbm, rr_hbm,
                upd, gl_out, gr_out, *scratch):
    scratch = list(scratch)
    take = lambda n: [scratch.pop(0) for _ in range(n)]
    gbf, zsend, zrecv = (take(PARTS) for _ in range(3))
    xret = take(NZ)
    (yown, yrecv, gsum, xsend, xrecv, gmat, dirb, xback, zback, zret, adam, gl, gr, rl, rr,
     gpart, gzrecv, gzsum, gxrecv, tbls,
     lsem, ysem, ysend_sem, yrecv_sem, zsend_sem, zrecv_sem, xsend_sem, xrecv_sem,
     bxsend_sem, bxrecv_sem, bzsend_sem, bzrecv_sem, gsend_sem, grecv_sem, osem) = scratch
    g, f, y, c, x, z = position()
    at_y = lambda i: (i * 2 + c, f)
    at_z = lambda i: (g, x * NZ + i)
    at_x = lambda i: (g, i * NZ + z)
    plus = lambda a, d, n: (a + d) % n
    sends = []

    def start(copy):
        copy.start()
        sends.append(copy)
        return copy

    own_copies = []
    for p in range(PARTS):
        copy = pltpu.make_async_copy(pairs.at[p, y], yown.at[p], ysem.at[p])
        copy.start()
        own_copies.append(copy)
    big = []
    for i, (src, dst) in enumerate(((adam_hbm.at[0], adam), (rl_hbm.at[0, 0], rl), (rr_hbm.at[0, 0], rr),
                                    (gl_hbm.at[0, 0], gl), (gr_hbm.at[0, 0], gr), (tbl_hbm, tbls))):
        copy = pltpu.make_async_copy(src, dst, lsem.at[i])
        copy.start()
        big.append(copy)

    barrier = pltpu.get_barrier_semaphore()
    partners = (
        [at_y(plus(y, d, NY)) for d in range(1, NY)]
        + [at_z(plus(z, d, NZ)) for d in range(1, NZ)]
        + [at_x(plus(x, d, NX)) for d in range(1, NX)]
    )
    for partner in partners:
        pl.semaphore_signal(barrier, inc=1, device_id=partner, device_id_type=MESH)
    pl.semaphore_wait(barrier, len(partners))

    y_copies = [[] for _ in range(PARTS)]
    for p in range(PARTS):
        for d in range(1, NY):
            to = plus(y, d, NY)
            y_copies[p].append(start(remote(
                pairs.at[p, to], yrecv.at[p, d - 1], ysend_sem.at[p * 3 + d - 1], yrecv_sem.at[p * 3 + d - 1], at_y(to))))

    z_copies = [[] for _ in range(PARTS)]
    x_copies = [[] for _ in range(PARTS)]

    def tbl(i):
        return tbls[0, i]

    def reduce_part(p):
        own_copies[p].wait()
        for copy in y_copies[p]:
            copy.wait_recv()
        total = yown[p].astype(jnp.float32)
        for d in range(NY - 1):
            total = total + yrecv[p, d].astype(jnp.float32)
        gsum[p] = total
        gbf[p][...] = total.astype(jnp.bfloat16)

        @pl.loop(0, NZ)
        def _(i):
            for k in range(cap):
                zsend[p][i, k] = gbf[p][tbl(T_LIST + i * 8 + k)]

        for d in range(1, NZ):
            to = plus(z, d, NZ)
            n = p * 7 + d - 1
            z_copies[p].append(start(remote(
                zsend[p].at[to], zrecv[p].at[z], zsend_sem.at[n], zrecv_sem.at[n], at_z(to))))
        zrecv[p][z] = zsend[p][z]

    def pass_on(p):
        for copy in z_copies[p]:
            copy.wait_recv()

        for i in range(NX * SLOTS):
            k = tbl(T_PLACE + i)
            for r in range(NZ):
                xsend[p, i // SLOTS, i % SLOTS, r] = zrecv[p][r, k]

        for d in range(1, NX):
            to = plus(x, d, NX)
            n = p * 3 + d - 1
            x_copies[p].append(start(remote(
                xsend.at[p, to], xrecv.at[p, x], xsend_sem.at[n], xrecv_sem.at[n], at_x(to))))
        xrecv[p, x] = xsend[p, x]

    def apply_roots(p):
        for copy in x_copies[p]:
            copy.wait_recv()

        @pl.loop(0, SLOTS)
        def _(s):
            block = xrecv[p, :, s].reshape(ORDER, COLS)
            gmat[s, :, p * COLS:(p + 1) * COLS] = block
            left = jnp.dot(rl[s], block, preferred_element_type=jnp.float32).astype(jnp.bfloat16)
            term = jnp.dot(left, rr[s, p * COLS:(p + 1) * COLS, :], preferred_element_type=jnp.float32)
            if p == 0:
                dirb[s] = term
            else:
                dirb[s] += term

    graft_z = []
    graft_x = []

    def graft_first():
        big[0].wait()
        part = jnp.zeros((BLOCKS, COLS), jnp.float32)
        for p in range(PARTS):
            total = gsum[p]
            second = BETA2 * adam[:, :, p * COLS:(p + 1) * COLS] + (1.0 - BETA2) * total * total
            ratio = total / (jnp.sqrt(second) + EPS_ADAM)
            part = part + jnp.sum(ratio * ratio, axis=1)
        gpart[...] = part
        for d in range(1, NZ):
            graft_z.append(start(remote(
                gpart, gzrecv.at[d - 1], gsend_sem.at[d - 1], grecv_sem.at[d - 1], at_z(plus(z, d, NZ)))))

    def graft_second():
        total = gpart[...]
        for d in range(NZ - 1):
            graft_z[d].wait_recv()
            total = total + gzrecv[d]
        gzsum[...] = total
        for d in range(1, NX):
            n = 6 + d
            graft_x.append(start(remote(
                gzsum, gxrecv.at[d - 1], gsend_sem.at[n], grecv_sem.at[n], at_x(plus(x, d, NX)))))

    big[5].wait()
    reduce_part(0)
    reduce_part(1)
    pass_on(0)
    reduce_part(2)
    pass_on(1)
    reduce_part(3)
    graft_first()
    big[1].wait()
    big[2].wait()
    apply_roots(0)
    pass_on(2)
    graft_second()
    apply_roots(1)
    pass_on(3)
    apply_roots(2)
    graft = gzsum[...]
    for d in range(NX - 1):
        graft_x[d].wait_recv()
        graft = graft + gxrecv[d]
    block_ids = lax.broadcasted_iota(jnp.int32, (BLOCKS, COLS), 0)
    graft_norms = []
    for s in range(SLOTS):
        graft_norms.append(jnp.sqrt(jnp.sum(jnp.where(block_ids == tbl(T_MINE + s), graft, 0.0), keepdims=True)))
    apply_roots(3)

    for s in range(SLOTS):
        whole = dirb[s]
        norm = jnp.sqrt(jnp.sum(whole * whole, keepdims=True))
        scale = -(graft_norms[s] / (norm + EPS_NORM))
        xback[:, s] = (whole * scale).astype(jnp.bfloat16).reshape(NX, NZ, ROWS, ORDER)
    bx_copies = [[] for _ in range(NZ)]
    bz_copies = []
    for d in BACK_ORDER:
        plane = plus(z, d, NZ)
        for e in range(1, NX):
            to = plus(x, e, NX)
            n = d * 3 + e - 1
            bx_copies[d].append(start(remote(
                xback.at[to, :, plane], xret[d].at[x], bxsend_sem.at[n], bxrecv_sem.at[n], at_x(to))))
        xret[d][x] = xback[x, :, plane]

    big[3].wait()
    big[4].wait()

    @pl.loop(0, SLOTS)
    def _(s):
        held = tbl(T_HELD + s) > 0
        block = gmat[s]
        outer = lax.dot_general(block, block, (((1,), (1,)), ((), ())), preferred_element_type=jnp.float32)
        gl_out[0, 0, s] = gl[s] + jnp.where(held, outer, 0.0)
        outer = lax.dot_general(block, block, (((0,), (0,)), ((), ())), preferred_element_type=jnp.float32)
        gr[s] = gr[s] + jnp.where(held, outer, 0.0)

    out_copy = pltpu.make_async_copy(gr, gr_out.at[0, 0], osem)
    out_copy.start()

    for d in BACK_ORDER:
        for copy in bx_copies[d]:
            copy.wait_recv()
        land = zback if d else zret
        for k in range(cap):
            e = tbl(T_OWNED + k)
            land[d, k] = xret[d][e // SLOTS, e % SLOTS]
        if d:
            bz_copies.append(start(remote(
                zback.at[d], zret.at[d], bzsend_sem.at[d - 1], bzrecv_sem.at[d - 1], at_z(plus(z, d, NZ)))))
    for copy in bz_copies:
        copy.wait_recv()
    for j in range(BLOCKS):
        away = (z + NZ - tbl(T_PLANE + j)) % NZ
        upd[0, j] = zret[away, tbl(T_RANK + j)]
    out_copy.wait()
    for copy in sends:
        copy.wait_send()


def step(cap, collective_id, tbl, pairs, adam_v, gram_left, gram_right, root_left, root_right):
    tile = (ROWS, COLS)
    bf, f32 = jnp.bfloat16, jnp.float32
    vm = pltpu.VMEM
    dma = pltpu.SemaphoreType.DMA
    scratch = (
        [vm((BLOCKS,) + tile, bf)] * PARTS
        + [vm((NZ, cap) + tile, bf)] * PARTS
        + [vm((NZ, cap) + tile, bf)] * PARTS
        + [vm((NX, SLOTS, ROWS, ORDER), bf)] * NZ
        + [
            vm((PARTS, BLOCKS) + tile, bf),
            vm((PARTS, NY - 1, BLOCKS) + tile, bf),
            vm((PARTS, BLOCKS) + tile, f32),
            vm((PARTS, NX, SLOTS, NZ) + tile, bf),
            vm((PARTS, NX, SLOTS, NZ) + tile, bf),
            vm((SLOTS, ORDER, ORDER), bf),
            vm((SLOTS, ORDER, ORDER), f32),
            vm((NX, SLOTS, NZ, ROWS, ORDER), bf),
            vm((NZ, cap, ROWS, ORDER), bf),
            vm((NZ, cap, ROWS, ORDER), bf),
            vm((BLOCKS, ROWS, ORDER), f32),
            vm((SLOTS, ORDER, ORDER), f32),
            vm((SLOTS, ORDER, ORDER), f32),
            vm((SLOTS, ORDER, ORDER), bf),
            vm((SLOTS, ORDER, ORDER), bf),
            vm((BLOCKS, COLS), f32),
            vm((NZ - 1, BLOCKS, COLS), f32),
            vm((BLOCKS, COLS), f32),
            vm((NX - 1, BLOCKS, COLS), f32),
            pltpu.SMEM((8, 128), jnp.int32),
            dma((6,)), dma((PARTS,)),
            dma((PARTS * 3,)), dma((PARTS * 3,)),
            dma((PARTS * 7,)), dma((PARTS * 7,)),
            dma((PARTS * 3,)), dma((PARTS * 3,)),
            dma((NZ * 3,)), dma((NZ * 3,)),
            dma((NZ - 1,)), dma((NZ - 1,)),
            dma((10,)), dma((10,)), dma,
        ]
    )
    hbm = pl.BlockSpec(memory_space=pl.ANY)
    return pl.pallas_call(
        functools.partial(step_kernel, cap),
        out_shape=(
            pltpu.VMEM((1, BLOCKS, ROWS, ORDER), bf),
            pltpu.VMEM(gram_left.shape, f32),
            jax.ShapeDtypeStruct(gram_right.shape, f32),
        ),
        in_specs=[hbm] * 7,
        out_specs=(pl.BlockSpec(memory_space=pltpu.VMEM), pl.BlockSpec(memory_space=pltpu.VMEM), hbm),
        scratch_shapes=scratch,
        compiler_params=pltpu.CompilerParams(
            collective_id=collective_id, has_side_effects=True, vmem_limit_bytes=32 << 20
        ),
        name=f"step_{cap}",
    )(tbl, pairs, adam_v, gram_left, gram_right, root_left, root_right)


def place_kernel(upd, gl, gr, upd_out, gl_out, gr_out, held, in_sem, out_sem):
    rows = ORDER // CHUNKS
    pieces = [(s, pl.ds(r * rows, rows)) for s in range(SLOTS) for r in range(CHUNKS)]
    loads = []
    for i, (s, r) in enumerate(pieces):
        copy = pltpu.make_async_copy(gr.at[0, 0, s, r], held.at[s, r], in_sem.at[i])
        copy.start()
        loads.append(copy)
    stores = [pltpu.make_async_copy(upd, upd_out, out_sem.at[0])]
    for i, (s, r) in enumerate(pieces):
        stores.append(pltpu.make_async_copy(gl.at[0, 0, s, r], gl_out.at[0, 0, s, r], out_sem.at[1 + i]))
    for copy in stores:
        copy.start()
    for i, (s, r) in enumerate(pieces):
        loads[i].wait()
        copy = pltpu.make_async_copy(held.at[s, r], gr_out.at[0, 0, s, r], out_sem.at[1 + len(pieces) + i])
        copy.start()
        stores.append(copy)
    for copy in stores:
        copy.wait()


def place(upd, gl, gr):
    hbm = pl.BlockSpec(memory_space=pl.ANY)
    vmem = pl.BlockSpec(memory_space=pltpu.VMEM)
    return pl.pallas_call(
        place_kernel,
        out_shape=tuple(jax.ShapeDtypeStruct(a.shape, a.dtype) for a in (upd, gl, gr)),
        in_specs=[hbm] * 3,
        out_specs=(hbm,) * 3,
        scratch_shapes=[
            pltpu.VMEM((SLOTS, ORDER, ORDER), jnp.float32),
            pltpu.SemaphoreType.DMA((SLOTS * CHUNKS,)),
            pltpu.SemaphoreType.DMA((SLOTS * CHUNKS * 2 + 1,)),
        ],
        compiler_params=pltpu.CompilerParams(vmem_limit_bytes=8 << 20),
        name="place",
    )(upd, gl, gr)


def per_device(grad_part, adam_v, owner_of, gram_left, gram_right, root_left, root_right):
    pairs, table, which = pair_sum(grad_part, owner_of.reshape(BLOCKS))
    operands = (table, pairs, adam_v, gram_left, gram_right, root_left, root_right)
    branches = [functools.partial(step, cap, i + 1) for i, cap in enumerate(CAPS)]
    return place(*lax.switch(which[0], branches, *operands))


def solution(mesh):
    placed = (
        P("grp", None, None, "fsdp", None),
        P("grp", None, "fsdp", None),
        P("grp", None, None),
        P("grp", "fsdp", None, None, None),
        P("grp", "fsdp", None, None, None),
        P("grp", "fsdp", None, None, None),
        P("grp", "fsdp", None, None, None),
    )
    return jax.shard_map(
        per_device,
        mesh=mesh,
        in_specs=placed,
        out_specs=(
            P("grp", None, "fsdp", None),
            P("grp", "fsdp", None, None, None),
            P("grp", "fsdp", None, None, None),
        ),
        check_vma=False,
    )
```

time: 99 us -> 70.1 us (0.71)
  Pallas kernels: 84.4 us -> 67.1 us
  local copies, waits for them, and re-layouts: 7.35 us -> 0.01 us
  other arithmetic: 4.46 us -> 0 us
    pallas_call x1 -> x2, Pallas kernels: 77.3 us -> 58.5 us  [the longest x1 55.1 us: step(): pl.pallas_call(functools.partial(step_kernel, cap), out_shape=(pltpu.VMEM...]
    unnamed x13 -> x4, local copies, waits for them, and re-layouts: 7.01 us -> 0.01 us
    reduce_sum x6 -> x0, other arithmetic: 1.74 us -> none  [the longest x2 1.09 us: index_table(): jnp.sum(jnp.where(same & earlier, 1, 0), axis=1).astype(jnp.int32)]
    eq x4 -> x0, other arithmetic: 1.41 us -> none  [the longest x1 0.73 us: index_table(): owner_ids == owners]
    pallas_call x1, Pallas kernels: 7.15 us -> 8.55 us  [pair_sum(): pl.pallas_call(pair_kernel, out_shape=(jax.ShapeDtypeStruct((PARTS, NY, B...]
where the time goes in v2:
time: 70.1 us; the launch traced here: 68.8 us
  Pallas kernels  67.1 us (96%)
  between operations  1.42 us (2%)
    pallas_call x1, Pallas kernels, step(): pl.pallas_call(functools.partial(step_kernel, cap), out_shape=(pltpu.VMEM...  55.1 us
    pallas_call x1, Pallas kernels, pair_sum(): pl.pallas_call(pair_kernel, out_shape=(jax.ShapeDtypeStruct((PARTS, NY, B...  8.55 us
    pallas_call x1, Pallas kernels, place(): pl.pallas_call(place_kernel, out_shape=tuple((jax.ShapeDtypeStruct(a.shap...  3.47 us

profile of v2, /device:TPU:4, one launch (start us, length us, event | category | flops | bytes accessed | tf_op | source)
XLA Modules:
  0.0 68.8 jit_solution(5625032981060683276)
XLA Ops:
  0.6 0.0 copy-start
  0.6 0.0 copy-start.1
  0.7 8.6 %pair_sum.1 = (bf16[4,4,16,16,128]{4,3,2,1,0:T(8,128)(2,1)}, s32[8,128]{1,0:T(8,128)S(1)}, s32[1]{0:T(128)}) custom-call(bf16[1,8,16,16,512]{4,3,2,1,0:T(8,128)(2,1)} %parts_ref.1, s32[16]{0:T(128)} %bitcast.2), custom_call_target="tpu_custom_call" | custom-call | tf_op jit(solution)/shard_map/pair_sum/pallas_call | solution.py:114
  9.8 0.0 copy-done
  9.8 0.0 copy-done.1
  9.8 55.3 %conditional.1 = ((bf16[1,16,16,512]{3,2,1,0:T(8,128)(2,1)S(1)}, f32[1,1,2,512,512]{4,3,2,1,0:T(8,128)S(1)}, f32[1,1,2,512,512]{4,3,2,1,0:T(8,128)})) conditional(s32[]{:T(128)} %bitcast.1, (s32[8,128]{1,0:T(8,128)S(1)}, bf16[4,4,16,16,128]{4,3,2,1,0:T(8,128)(2,1)}, f32[1,16,16,512]{3,2,1,0:T(8,128)S(1)}, ...), branch_computations={%region_0.0_spmd, %region_1.0_spmd, %region_2.0_spmd} | conditional | bytes 8 | solution.py:461
  9.8 55.1 %step_4.1 = (bf16[1,16,16,512]{3,2,1,0:T(8,128)(2,1)S(1)}, f32[1,1,2,512,512]{4,3,2,1,0:T(8,128)S(1)}, f32[1,1,2,512,512]{4,3,2,1,0:T(8,128)}) custom-call(s32[8,128]{1,0:T(8,128)S(1)} %get-tuple-element.42.tbl_hbm, bf16[4,4,16,16,128]{4,3,2,1,0:T(8,128)(2,1)} %get-tuple-element.43.pairs, f32[1,16,16,512]{3,2,1,0:T(8,128)S(1)} %get-tuple-element.44.adam_hbm, ...), custom_call_target="tpu_custom_call" | custom-call | tf_op jit(solution)/shard_map/cond/branch_0_fun/step_4/pallas_call | solution.py:400
  65.1 3.5 %place.1 = (bf16[1,16,16,512]{3,2,1,0:T(8,128)(2,1)}, f32[1,1,2,512,512]{4,3,2,1,0:T(8,128)}, f32[1,1,2,512,512]{4,3,2,1,0:T(8,128)}) custom-call(bf16[1,16,16,512]{3,2,1,0:T(8,128)(2,1)S(1)} %get-tuple-element.75.upd, f32[1,1,2,512,512]{4,3,2,1,0:T(8,128)S(1)} %get-tuple-element.76.gl, f32[1,1,2,512,512]{4,3,2,1,0:T(8,128)} %get-tuple-element.77.gr), custom_call_target="tpu_custom_call" | custom-call | tf_op jit(solution)/shard_map/place/pallas_call | solution.py:442
Async XLA Ops:
  0.6 9.1 %copy-start = (bf16[1,1,2,512,512]{4,3,2,1,0:T(8,128)(2,1)S(1)}, bf16[1,1,2,512,512]{4,3,2,1,0:T(8,128)(2,1)}, u32[]{:S(2)}) copy-start(bf16[1,1,2,512,512]{4,3,2,1,0:T(8,128)(2,1)} %param.15) | copy-start | bytes 3145732
  0.6 9.1 %copy-start.1 = (f32[1,16,16,512]{3,2,1,0:T(8,128)S(1)}, f32[1,16,16,512]{3,2,1,0:T(8,128)}, u32[]{:S(2)}) copy-start(f32[1,16,16,512]{3,2,1,0:T(8,128)} %param.11) | copy-start | bytes 1572868
